TPU v7x, 512 devices: a whole 4x4x16 slice. The times are simulated.
512 devices in a mesh: helpers: 64 (over y_lo, z, core), subtree: 8 (over y_hi, x).
Axes of the slice: x: 4, y: 4 (y_hi: 2, y_lo: 2; y = y_hi * 2 + y_lo), z: 16, core: 2. Of those that a mesh axis runs over, the one named last changes fastest.
Arguments:
- child_fronts: bfloat16 [8192, 65536], P('helpers', 'subtree'), may hold values from -3 to 3
- parent_front: bfloat16 [8192, 8192], P('helpers', 'subtree'), may hold values from -3 to 3
- child_inverse: bfloat16 [8, 128, 128], P('subtree'), may hold values from -0.046875 to 0.046875
- parent_inverse: bfloat16 [256, 256], replicated, may hold values from -0.0234375 to 0.0234375
- helper_plan: int32 [8, 64], P('subtree'), may hold values from 0 to 63, as said below
- child_map: int32 [8, 8192], P('subtree'), may hold values from 0 to 8191, as said below
- child_orders: int32 [8], P('subtree'), may hold values from 4096 to 8192
- child_pivots: int32 [8], P('subtree'), may hold values from 64 to 128
- parent_pivots: int32 [1], replicated, may hold values from 128 to 256
Outputs:
- parent_schur: bfloat16 [8192, 8192], P('helpers', 'subtree')
Inputs may be any that keep to these rules, and one draw needn't show every extreme that they name: `helper_plan`: each row is a permutation of 0 to 63. `child_map`: each row is a permutation of 0 to 8191; an index of child front s in row block helper_plan[s, h] maps into parent indices h * (128) to (h + 1) * 128 - 1.
All inputs are finite; a program needn't handle non-finite values.
Results may differ from a plain program's by a relative error of at most 0.017.
Values may be sent and summed in bfloat16 or wider, within the bound.
A program may use at most 64 MiB of HBM per device.

v0:
```python
import jax
import jax.numpy as jnp
from jax import lax
from jax.sharding import Mesh
from jax.sharding import PartitionSpec as P

P1 = 128
P2 = 256
HELPERS = ("helpers_0", "helpers_1", "helpers_2")


def broadcast_by_axis(shard, axes, root):
    shard = jnp.where(lax.axis_index(axes) == root, shard, jnp.zeros_like(shard))
    for axis in axes:
        shard = lax.psum(shard, axis)
    return shard


def in_blocks(shard, dim, size):
    before, after = (shard.shape[:dim], shard.shape[dim + 1 :])
    return jnp.moveaxis(shard.reshape(*before, size, -1, *after), dim, 0)


def sent_and_summed(shard, axis, dim):
    size = lax.axis_size(axis)
    pieces = lax.all_to_all(in_blocks(shard, dim, size), axis, 0, 0, tiled=True)
    return jnp.sum(pieces.astype(jnp.float32), axis=0)


def copy_for_each(shard, axis):
    size = lax.axis_size(axis)
    return lax.all_to_all(
        jnp.broadcast_to(shard[None], (size, *shard.shape)), axis, 0, 0, tiled=True
    )


def of_everyone(shard, axis):
    everything = copy_for_each(shard, axis)
    return jnp.sum(everything.astype(jnp.float32), axis=0)


def picked(shard, axis, root):
    return lax.dynamic_index_in_dim(lax.all_gather(shard, axis), root, 0, keepdims=False)


def local(
    child_fronts,
    parent_front,
    child_inverse,
    parent_inverse,
    helper_plan,
    child_map,
    child_orders,
    child_pivots,
    parent_pivots,
):
    row_count, front_width = child_fronts.shape
    helper = lax.axis_index(HELPERS)
    helpers = lax.axis_size(HELPERS)
    helper_ids = jnp.arange(helpers, dtype=jnp.int32)
    plan_row = helper_plan[0]
    own_block = jnp.sum(jnp.where(helper_ids == helper, plan_row, 0))
    front_order = child_orders[0]
    columns = jnp.arange(front_width, dtype=jnp.int32)
    local_index = own_block * row_count + jnp.arange(row_count, dtype=jnp.int32)
    live_cols = columns < front_order
    live_rows = local_index < front_order
    zero_value = jnp.zeros((), jnp.bfloat16)
    front_local = jnp.where(live_rows[:, None] & live_cols[None, :], child_fronts, zero_value)
    multipliers = jnp.dot(front_local[:, :P1], child_inverse[0], preferred_element_type=jnp.float32)
    multipliers = jnp.where(
        columns[:P1][None, :] < child_pivots[0], multipliers, jnp.zeros((), jnp.float32)
    ).astype(jnp.bfloat16)
    schur_rows = front_local.astype(jnp.float32)
    turn_index = 0
    root_helper = jnp.sum(jnp.where(plan_row == turn_index, helper_ids, 0))
    pivot_panel = broadcast_by_axis(child_fronts, HELPERS, root_helper)
    pivot_panel = jnp.where(live_cols[None, :], pivot_panel, zero_value)
    schur_rows = schur_rows - jnp.dot(multipliers, pivot_panel, preferred_element_type=jnp.float32)
    contribution = schur_rows.astype(jnp.bfloat16)
    source = jnp.zeros((front_width,), jnp.int32).at[child_map[0]].set(columns)
    accepted = (source >= P1) & (source < front_order)
    local_source = (
        lax.dynamic_slice_in_dim(source, helper * row_count, row_count) - own_block * row_count
    )
    local_accepted = lax.dynamic_slice_in_dim(accepted, helper * row_count, row_count)
    extended = jnp.take(jnp.take(contribution, local_source, axis=0), source, axis=1).astype(
        jnp.float32
    )
    extended = jnp.where(
        local_accepted[:, None] & accepted[None, :], extended, jnp.zeros((), jnp.float32)
    )
    summed = sent_and_summed(extended.astype(jnp.bfloat16), "subtree", 1)
    assembled = (parent_front.astype(jnp.float32) + summed).astype(jnp.bfloat16)
    on_first = lax.axis_index("subtree") == 0
    anchor = jnp.where(
        on_first, parent_front[:, :P2].astype(jnp.float32), jnp.zeros((), jnp.float32)
    )
    pieces = (
        of_everyone(extended[:, :P2].astype(jnp.bfloat16), "subtree").astype(jnp.float32),
        of_everyone(anchor.astype(jnp.bfloat16), "subtree").astype(jnp.float32),
    )
    pivot_cols = (pieces[1] + pieces[0]).astype(jnp.bfloat16)
    block_count = (P2 + row_count - 1) // row_count
    gathered = []
    for turn_index in range(block_count):
        gathered.append(picked(assembled, HELPERS, turn_index))
    pivot_rows = jnp.concatenate(gathered, axis=0)
    parent_mult = jnp.dot(pivot_cols, parent_inverse, preferred_element_type=jnp.float32)
    pivot_ids = jnp.arange(P2, dtype=jnp.int32)
    parent_mult = jnp.where(
        pivot_ids[None, :] < parent_pivots[0], parent_mult, jnp.zeros((), jnp.float32)
    ).astype(jnp.bfloat16)
    updated = assembled.astype(jnp.float32) - jnp.dot(
        parent_mult, pivot_rows, preferred_element_type=jnp.float32
    )
    return updated.astype(jnp.bfloat16)


def solution(mesh):
    torus = Mesh(
        mesh.devices.reshape(2, 16, 2, mesh.shape["subtree"]),
        ("helpers_0", "helpers_1", "helpers_2", "subtree"),
    )
    in_specs = (
        P(HELPERS, "subtree"),
        P(HELPERS, "subtree"),
        P("subtree", None, None),
        P(),
        P("subtree", None),
        P("subtree", None),
        P("subtree"),
        P("subtree"),
        P(),
    )
    out_specs = P(HELPERS, "subtree")
    return jax.shard_map(local, mesh=torus, in_specs=in_specs, out_specs=out_specs, check_vma=False)
```

profile of v0, /device:TPU:7, one launch (start us, length us, event | category | flops | bytes accessed | tf_op | source)
XLA Modules:
  0.0 524.6 jit_solution(2283298313270859373)
XLA Ops:
  7.2 1.4 fusion.21
  10.0 4.6 broadcast_select_fusion.1
  14.6 89.5 %all-reduce.4.cloned.1.call-done = bf16[128,8192]{1,0:T(8,128)(2,1)} async-done(((bf16[128,8192]{1,0:T(8,128)(2,1)}), bf16[128,8192]{1,0:T(8,128)(2,1)}) %all-reduce.4.cloned.1.call-update) | async-done | bytes 2097168 | tf_op jit(solution)/shard_map/psum | solution.py:15
  104.8 138.3 %all-reduce.6.cloned.1.call-done = bf16[128,8192]{1,0:T(8,128)(2,1)} async-done(((bf16[128,8192]{1,0:T(8,128)(2,1)}), bf16[128,8192]{1,0:T(8,128)(2,1)}) %all-reduce.6.cloned.1.call-update) | async-done | bytes 2097168 | tf_op jit(solution)/shard_map/psum | solution.py:15
  243.3 30.5 %scatter_custom_fusion = s32[8192]{0:T(1024)S(1)} fusion(s32[8192]{0:T(1024)S(1)} %bitcast.30, s32[8192]{0:T(1024)S(1)} %iota.24, s32[]{:T(128)} %constant.31.clone.1), kind=kCustom, calls=%fused_computation.41 | custom fusion | bytes 32772 | tf_op jit(solution)/shard_map/scatter | solution.py:81
  274.0 19.7 %all-reduce.8.cloned.1.call-done = bf16[128,8192]{1,0:T(8,128)(2,1)} async-done(((bf16[128,8192]{1,0:T(8,128)(2,1)}), bf16[128,8192]{1,0:T(8,128)(2,1)}) %all-reduce.8.cloned.1.call-update) | async-done | bytes 2097168 | tf_op jit(solution)/shard_map/psum | solution.py:15
  293.7 3.1 fusion
  296.8 3.2 gather_fusion
  300.0 3.2 broadcast_select_fusion
  303.2 3.2 copy.17
  306.5 29.2 %gather_fusion.1 = bf16[8192,128]{1,0:T(8,128)(2,1)} fusion(bf16[128,8192]{0,1:T(8,128)(2,1)S(1)} %copy.17, s32[8192]{0:T(1024)S(1)} %fusion.17), kind=kCustom, calls=%fused_computation.1 | custom fusion | bytes 4227072 | tf_op jit(solution)/shard_map/jit(_take)/gather | solution.py:87
  335.7 2.9 copy.18
  338.6 1.0 fusion.1
  339.6 32.1 %all_to_all.15 = bf16[8,128,1024]{2,1,0:T(8,128)(2,1)S(1)} all-to-all(bf16[8,128,1024]{2,1,0:T(8,128)(2,1)S(1)} %fusion.1), channel_id=1, replica_groups=mesh['helpers_0'=2,'helpers_1'=16,'helpers_2'=2,'subtree'=8] {'subtree'}, dimensions={0} | all-to-all | bytes 4194304 | tf_op jit(solution)/shard_map/all_to_all | solution.py:26
  372.1 0.6 copy-done.2
  372.7 0.8 add_convert_fusion
  373.5 0.8 broadcast_in_dim.112
  374.3 6.6 %all-to-all-start.1 = ((bf16[8,128,256]{2,1,0:T(8,128)(2,1)}), bf16[8,128,256]{2,1,0:T(8,128)(2,1)S(1)}, u32[]{:S(2)}, u32[]{:S(2)}) async-start(bf16[8,128,256]{2,1,0:T(8,128)(2,1)} %broadcast_in_dim.112), calls=%async_computation.1 | async-start | bytes 1048576 | tf_op jit(solution)/shard_map/all_to_all | solution.py:32
  381.0 7.6 %all-to-all-done.1 = bf16[8,128,256]{2,1,0:T(8,128)(2,1)S(1)} async-done(((bf16[8,128,256]{2,1,0:T(8,128)(2,1)}), bf16[8,128,256]{2,1,0:T(8,128)(2,1)S(1)}, u32[]{:S(2)}, u32[]{:S(2)}) %all-to-all-start.1) | async-done | bytes 524320 | tf_op jit(solution)/shard_map/all_to_all | solution.py:32
  388.5 0.8 broadcast_in_dim.115
  389.4 7.5 %all-to-all-start.2 = ((bf16[8,128,256]{2,1,0:T(8,128)(2,1)}), bf16[8,128,256]{2,1,0:T(8,128)(2,1)S(1)}, u32[]{:S(2)}, u32[]{:S(2)}) async-start(bf16[8,128,256]{2,1,0:T(8,128)(2,1)} %broadcast_in_dim.115), calls=%async_computation.2 | async-start | bytes 1048576 | tf_op jit(solution)/shard_map/all_to_all | solution.py:32
  397.6 9.8 %all-to-all-done.2 = bf16[8,128,256]{2,1,0:T(8,128)(2,1)S(1)} async-done(((bf16[8,128,256]{2,1,0:T(8,128)(2,1)}), bf16[8,128,256]{2,1,0:T(8,128)(2,1)S(1)}, u32[]{:S(2)}, u32[]{:S(2)}) %all-to-all-start.2) | async-done | bytes 524320 | tf_op jit(solution)/shard_map/all_to_all | solution.py:32
  407.5 108.5 %all-gather.3.cloned.1.call-done = bf16[8192,1024]{1,0:T(8,128)(2,1)} async-done(((bf16[128,1024]{1,0:T(8,128)(2,1)}), bf16[8192,1024]{1,0:T(8,128)(2,1)}) %all-gather.3.cloned.1.call-update) | async-done | bytes 16777232 | tf_op jit(solution)/shard_map/all_gather | solution.py:43
  516.0 2.1 fusion.4
  (37 shorter events, 1.1 us)
Async XLA Ops:
  6.5 509.4 %copy-start = (bf16[256,256]{1,0:T(8,128)(2,1)S(1)}, bf16[256,256]{1,0:T(8,128)(2,1)}, u32[]{:S(2)}) copy-start(bf16[256,256]{1,0:T(8,128)(2,1)} %param.12) | copy-start | bytes 393220
  6.5 97.5 %all-reduce.4.cloned.1.call-start = ((), (), s32[]{:S(2)}) async-start(), calls=%async_computation.3 | async-start | bytes 4194304 | tf_op jit(solution)/shard_map/psum | solution.py:15
  14.6 228.6 %all-reduce.6.cloned.1.call-start = ((), (), s32[]{:S(2)}) async-start(), calls=%async_computation.4 | async-start | bytes 4194304 | tf_op jit(solution)/shard_map/psum | solution.py:15
  104.1 139.1 %copy-start.3 = (s32[1,8192]{1,0:T(1,128)S(1)}, s32[1,8192]{1,0:T(1,128)}, u32[]{:S(2)}) copy-start(s32[1,8192]{1,0:T(1,128)} %param.14) | copy-start | bytes 98308
  104.1 189.7 %copy-start.4 = (bf16[1,128,128]{2,1,0:T(8,128)(2,1)S(1)}, bf16[1,128,128]{2,1,0:T(8,128)(2,1)}, u32[]{:S(2)}) copy-start(bf16[1,128,128]{2,1,0:T(8,128)(2,1)} %param.11) | copy-start | bytes 98308
  104.1 189.6 %all-reduce.8.cloned.1.call-start = ((), (), s32[]{:S(2)}) async-start(), calls=%async_computation.5 | async-start | bytes 4194304 | tf_op jit(solution)/shard_map/psum | solution.py:15
  243.2 272.8 %all-gather.3.cloned.1.call-start = ((), (), s32[]{:S(2)}) async-start(), calls=%async_computation.6 | async-start | bytes 17039360 | tf_op jit(solution)/shard_map/all_gather | solution.py:43
  371.7 1.0 copy-start.2
  374.3 141.7 %copy-start.1 = (bf16[128,1024]{1,0:T(8,128)(2,1)S(1)}, bf16[128,1024]{1,0:T(8,128)(2,1)}, u32[]{:S(2)}) copy-start(bf16[128,1024]{1,0:T(8,128)(2,1)} %add_convert_fusion) | copy-start | bytes 786436
  374.3 14.2 %all-to-all-start.1 = ((bf16[8,128,256]{2,1,0:T(8,128)(2,1)}), bf16[8,128,256]{2,1,0:T(8,128)(2,1)S(1)}, u32[]{:S(2)}, u32[]{:S(2)}) async-start(bf16[8,128,256]{2,1,0:T(8,128)(2,1)} %broadcast_in_dim.112), calls=%async_computation.1 | async-start | bytes 1048576 | tf_op jit(solution)/shard_map/all_to_all | solution.py:32
  389.4 18.0 %all-to-all-start.2 = ((bf16[8,128,256]{2,1,0:T(8,128)(2,1)}), bf16[8,128,256]{2,1,0:T(8,128)(2,1)S(1)}, u32[]{:S(2)}, u32[]{:S(2)}) async-start(bf16[8,128,256]{2,1,0:T(8,128)(2,1)} %broadcast_in_dim.115), calls=%async_computation.2 | async-start | bytes 1048576 | tf_op jit(solution)/shard_map/all_to_all | solution.py:32
Sparse Core Ops, SparseCore 0:
  14.7 89.3 all-reduce.3
  106.5 136.5 all-reduce.5
  246.3 47.4 all-reduce.7
  373.6 142.3 all-gather.2
where the time goes:
time: 525 us
  waiting for transfers between devices  373 us (71%)
  local copies, waits for them, and re-layouts  71.4 us (14%)
  blocking collectives  32.1 us (6%)
  between operations  16.6 us (3%)
  starting transfers between devices  14.2 us (3%)
  other arithmetic  11.7 us (2%)
    psum x3, waiting for transfers between devices, broadcast_by_axis(): shard = lax.psum(shard, axis)  248 us
    all_gather x1, waiting for transfers between devices, picked(): lax.all_gather(shard, axis)  109 us
    gather x2, local copies, waits for them, and re-layouts, local(): jnp.take(jnp.take(contribution, local_source, axis=0), source, axis=1)  32.1 us
    all_to_all x1, blocking collectives, sent_and_summed(): pieces = lax.all_to_all(in_blocks(shard, dim, size), axis, 0, 0, tiled=True)  32.1 us
    scatter x1, local copies, waits for them, and re-layouts, local(): source = jnp.zeros((front_width,), jnp.int32).at[child_map[0]].set(columns)  30.5 us
    all_to_all x2, waiting for transfers between devices, copy_for_each(): lax.all_to_all(jnp.broadcast_to(shard[None], (size, *shard.shape)), axis,...  17.4 us
    all_to_all x2, starting transfers between devices, copy_for_each(): lax.all_to_all(jnp.broadcast_to(shard[None], (size, *shard.shape)), axis,...  14.1 us
  transfers between devices with their start and end apart: 6, of which 6 were waited for; matrix products, arithmetic and copies ran while one was open for 6% of the time, Pallas kernels for 0%

commit v1 on v0

v1 whole, which is shorter than its diff:
```python
import functools

import jax
import jax.numpy as jnp
from jax import lax
from jax.experimental import pallas as pl
from jax.experimental.pallas import tpu as pltpu
from jax.sharding import PartitionSpec as P

MESH = pl.DeviceIdType.MESH
BF16 = jnp.bfloat16
F32 = jnp.float32
B = 128
S = 8
Z = 16
W = 1024
P2 = 256
SUBS = 2


def permute_kernel(h_ref, plan_ref, order_ref, pivots_ref, map_ref, front_ref, inv_ref, a_ref, panel_ref, m_ref):
    h = h_ref[0]
    order = order_ref[0]
    rows = lax.broadcasted_iota(jnp.int32, (B, B), 0)
    lanes = lax.broadcasted_iota(jnp.int32, (1, B), 1)

    def selector(j):
        block = plan_ref[0, j]
        place = map_ref[:, pl.ds(pl.multiple_of(block * B, B), B)] - j * B
        index = block * B + lanes
        place = jnp.where((index >= B) & (index < order), place, -1)
        return jnp.where(rows == place, 1.0, 0.0).astype(BF16)

    own = selector(h)
    root = plan_ref[0, h] == 0
    m = jnp.dot(front_ref[:, :B], inv_ref[0], preferred_element_type=F32)
    m = jnp.where(lanes < pivots_ref[0], m, 0.0).astype(BF16)
    m_ref[...] = jnp.dot(own, m, preferred_element_type=F32).astype(BF16)

    @pl.loop(0, S)
    def _(c):
        for i in range(W // B):
            j = c * (W // B) + i
            block = plan_ref[0, j]
            x = front_ref[:, pl.ds(pl.multiple_of(block * B, B), B)]
            x = lax.dot_general(x, selector(j), (((1,), (1,)), ((), ())), preferred_element_type=F32).astype(BF16)
            a_ref[c, :, i * B : (i + 1) * B] = jnp.dot(own, x, preferred_element_type=F32).astype(BF16)
            x = jnp.where(root, x, jnp.zeros_like(x))
            for r in range(B // 16):
                p = r * 4 + i // 2
                panel_ref[p // Z, p % Z, c, :, (i % 2) * B : (i % 2 + 1) * B] = x[r * 16 : (r + 1) * 16]


def exchange_kernel(
    a_ref, panel_ref, m_ref, parent_ref, pinv_ref, pp_ref, o_ref,
    sib, part, up_buf, dn_buf, piece, spread, slots, mb, a_in, m_in, raw, lhs, rhs, asm, prow, pm,
    a_s, a_r, m_s, m_r, sib_s, sib_r, rs_s, rs_r, sp_s, sp_r, sc_s, sc_r, ag_s, ag_r, fw_s, fw_r, pm_s, pm_r,
):
    h = lax.axis_index("helpers")
    s = lax.axis_index("subtree")
    y, z, k = h // (2 * Z), (h // 2) % Z, h % 2

    def at(y, z, k):
        return y * (2 * Z) + z * 2 + k

    up = (at(y, (z + 1) % Z, k), s)
    dn = (at(y, (z + Z - 1) % Z, k), s)
    sibling = (at(y, z, 1 - k), s)
    plane = [(dy, d) for dy in range(2) for d in range(S) if dy or d]
    first = jnp.logical_and(y == 0, z == 0)

    def plane_peer(dy, d):
        return (at((y + dy) % 2, z, k), (s + d) % S)

    def remote(src, dst, send, recv, device):
        copy = pltpu.make_async_remote_copy(
            src_ref=src, dst_ref=dst, send_sem=send, recv_sem=recv, device_id=device, device_id_type=MESH
        )
        return copy

    barrier = pltpu.get_barrier_semaphore()
    peers = [up, dn, sibling] + [plane_peer(*e) for e in plane]
    for peer in peers:
        pl.semaphore_signal(barrier, inc=1, device_id=peer, device_id_type=MESH)

    @pl.when(jnp.logical_not(first))
    def _():
        pl.semaphore_signal(barrier, inc=1, device_id=(at(0, 0, k), s), device_id_type=MESH)

    pl.semaphore_wait(barrier, len(peers) + jnp.where(first, 2 * Z - 1, 0))

    cross = remote(panel_ref.at[1 - k], sib, sib_s.at[0], sib_r.at[0], sibling)
    cross.start()
    m_copies, a_copies = [], []
    for d in range(1, S):
        m_copies.append(remote(m_ref, m_in.at[d], m_s.at[d], m_r.at[d], (h, (s + d) % S)))
        m_copies[-1].start()
    for d in range(1, S):
        a_copies.append(remote(a_ref.at[(s + d) % S], a_in.at[d], a_s.at[d], a_r.at[d], (h, (s + d) % S)))
        a_copies[-1].start()
    cross.wait_recv()

    @pl.loop(0, Z)
    def _(j):
        part[j] = panel_ref[k, j] + sib[j]

    halves = S // SUBS

    def finish_sums():
        for copy in m_copies + a_copies:
            copy.wait_recv()

        @pl.loop(0, B // 16)
        def _(g):
            rows = pl.ds(pl.multiple_of(g * 16, 16), 16)
            total = parent_ref[rows].astype(F32) + a_ref[s, rows].astype(F32)
            for d in range(1, S):
                total += a_in[d, rows].astype(F32)
            raw[rows] = total
            rounded = total.astype(BF16)
            for q in range(4):
                mb[g * 2 + q // 2, 32 + (q % 2) * 16 : 48 + (q % 2) * 16] = rounded[:, q * P2 : (q + 1) * P2]

        lhs[:B, pl.ds(pl.multiple_of(s * B, B), B)] = m_ref[...]
        for d in range(1, S):
            lhs[:B, pl.ds(pl.multiple_of((s + S - d) % S * B, B), B)] = m_in[d]
        for j in range(Z):
            for i in range(2):
                top = (j % 2) * 64 + i * 32
                mb[j, :32, i * B : (i + 1) * B] = lhs[top : top + 32, (j // 2) * B : (j // 2 + 1) * B]

    rs = {}
    rs_all = []
    for t in range(8):
        if t == 6:
            finish_sums()
        for i in range(SUBS):
            cut = pl.ds(i * halves, halves)
            for way, (buf, peer) in enumerate(((up_buf, up), (dn_buf, dn))):
                j = (z + 8 - t) % Z if way == 0 else (z + Z - 7 + t) % Z
                if way == 1 and t == 7:
                    continue
                if t == 0:
                    src = part.at[j, cut]
                else:
                    rs[way, i].wait_recv()
                    buf[t - 1, cut] = buf[t - 1, cut] + part[j, cut]
                    src = buf.at[t - 1, cut]
                rs[way, i] = remote(src, buf.at[t, cut], rs_s.at[way, t, i], rs_r.at[way, t, i], peer)
                rs[way, i].start()
                rs_all.append(rs[way, i])

    own_slot = k * Z + z

    @pl.when(first)
    def _():
        for e in range(1, 2 * Z):
            remote(
                mb.at[e % Z], slots.at[k * Z + e % Z, pl.ds(B, 64)], sc_s.at[e], sc_r.at[0], (at(e // Z, e % Z, k), s)
            ).start()
        slots[k * Z, B:] = mb[0]

    for i in range(SUBS):
        rs[0, i].wait_recv()
        rs[1, i].wait_recv()
    piece[...] = part[z] + up_buf[7] + dn_buf[6]

    spreads = {}
    for dy, d in plane:
        spreads[dy, d] = remote(
            piece.at[(s + d) % S], spread.at[dy, d], sp_s.at[dy, d], sp_r.at[dy, d], plane_peer(dy, d)
        )
        spreads[dy, d].start()
    for e in plane:
        spreads[e].wait_recv()
    for d in range(S):
        source = (s + S - d) % S
        mine = piece[s] if d == 0 else spread[0, d]
        slots[own_slot, pl.ds(pl.multiple_of(source * 16, 16), 16)] = mine + spread[1, d]

    @pl.when(jnp.logical_not(first))
    def _():
        remote(mb.at[0], slots.at[own_slot, pl.ds(B, 64)], sc_s.at[0], sc_r.at[0], sibling).wait_recv()

    height = (B + 64) // SUBS
    ag, ag_all, forwards = {}, [], []

    def ring(t, way, i, j, peer):
        ref = slots.at[k * Z + j, pl.ds(i * height, height)]
        ag[way, i] = remote(ref, ref, ag_s.at[way, t, i], ag_r.at[way, t, i], peer)
        ag[way, i].start()
        ag_all.append(ag[way, i])

    def forward(n, j):
        ref = slots.at[k * Z + j]
        forwards.append(remote(ref, ref, fw_s.at[n], fw_r.at[n], sibling))
        forwards[-1].start()

    for t in range(9):
        for i in range(SUBS):
            for way, peer in ((0, up), (1, dn)):
                j = (z + Z - t) % Z if way == 0 else (z + t) % Z
                if t > 0 and not (way == 1 and t == 8):
                    ag[way, i].wait_recv()
                if t < 8 - way:
                    ring(t, way, i, j, peer)
        forward(t, (z + Z - t) % Z)
        if 0 < t < 8:
            forward(8 + t, (z + t) % Z)
    for copy in forwards:
        copy.wait_recv()

    for p in range(2 * Z):
        for i in range(S):
            rhs[p % 4, i * B + (p // 4) * 16 : i * B + (p // 4 + 1) * 16] = slots[p, i * 16 : (i + 1) * 16]
        for i in range(2):
            top = B + (p // Z) * B + (p % 2) * 64 + i * 32
            left = (p % Z) // 2 * B
            lhs[top : top + 32, left : left + B] = slots[p, B : B + 32, i * B : (i + 1) * B]

    def assemble(q):
        cols = slice(q * P2, (q + 1) * P2)
        update = jnp.dot(lhs[...], rhs[q], preferred_element_type=F32)
        asm[:, cols] = (raw[:, cols] - update[:B]).astype(BF16)
        for p in range(Z):
            place = (p // 8) * Z + (p % 8) * 2 + q // 2
            base = slots[place, B + 32 + (q % 2) * 16 : B + 48 + (q % 2) * 16].astype(F32)
            prow[p * 16 : (p + 1) * 16, cols] = (base - update[B + p * 16 : B + (p + 1) * 16]).astype(BF16)

    assemble(0)

    def pm_copy(d):
        return remote(pm, pm, pm_s.at[d], pm_r.at[0], (h, (s + d) % S))

    @pl.when(s == 0)
    def _():
        m = jnp.dot(asm[:, :P2], pinv_ref[...], preferred_element_type=F32)
        lanes = lax.broadcasted_iota(jnp.int32, (1, P2), 1)
        pm[...] = jnp.where(lanes < pp_ref[0], m, 0.0).astype(BF16)
        for d in range(1, S):
            pm_copy(d).start()

    for q in range(1, 4):
        assemble(q)

    @pl.when(s != 0)
    def _():
        pm_copy(1).wait_recv()

    for q in range(4):
        cols = slice(q * P2, (q + 1) * P2)
        update = jnp.dot(pm[...], prow[:, cols], preferred_element_type=F32)
        o_ref[:, cols] = (asm[:, cols].astype(F32) - update).astype(BF16)

    for copy in [cross] + m_copies + a_copies + rs_all + list(spreads.values()) + ag_all + forwards:
        copy.wait_send()

    @pl.when(first)
    def _():
        for e in range(1, 2 * Z):
            remote(
                mb.at[e % Z], slots.at[k * Z + e % Z, pl.ds(B, 64)], sc_s.at[e], sc_r.at[0], (at(e // Z, e % Z, k), s)
            ).wait_send()

    @pl.when(s == 0)
    def _():
        for d in range(1, S):
            pm_copy(d).wait_send()


def local(
    child_fronts,
    parent_front,
    child_inverse,
    parent_inverse,
    helper_plan,
    child_map,
    child_orders,
    child_pivots,
    parent_pivots,
):
    h = jnp.reshape(lax.axis_index("helpers"), (1,)).astype(jnp.int32)
    smem = pl.BlockSpec(memory_space=pltpu.SMEM)
    vmem = pl.BlockSpec(memory_space=pltpu.VMEM)
    a, panel, m = pl.pallas_call(
        permute_kernel,
        out_shape=(
            jax.ShapeDtypeStruct((S, B, W), BF16),
            jax.ShapeDtypeStruct((2, Z, S, 16, P2), BF16),
            jax.ShapeDtypeStruct((B, B), BF16),
        ),
        in_specs=[smem] * 4 + [vmem] * 3,
        out_specs=(vmem, vmem, vmem),
        compiler_params=pltpu.CompilerParams(vmem_limit_bytes=32 << 20),
        name="permute",
    )(h, helper_plan, child_orders, child_pivots, child_map, child_fronts, child_inverse)
    dma = pltpu.SemaphoreType.DMA
    return pl.pallas_call(
        exchange_kernel,
        out_shape=jax.ShapeDtypeStruct((B, W), BF16),
        in_specs=[vmem] * 5 + [smem],
        out_specs=vmem,
        scratch_shapes=[
            pltpu.VMEM((Z, S, 16, P2), BF16),
            pltpu.VMEM((Z, S, 16, P2), BF16),
            pltpu.VMEM((8, S, 16, P2), BF16),
            pltpu.VMEM((7, S, 16, P2), BF16),
            pltpu.VMEM((S, 16, P2), BF16),
            pltpu.VMEM((2, S, 16, P2), BF16),
            pltpu.VMEM((2 * Z, B + 64, P2), BF16),
            pltpu.VMEM((Z, 64, P2), BF16),
            pltpu.VMEM((S, B, W), BF16),
            pltpu.VMEM((S, B, B), BF16),
            pltpu.VMEM((B, W), F32),
            pltpu.VMEM((B + P2, S * B), BF16),
            pltpu.VMEM((4, S * B, P2), BF16),
            pltpu.VMEM((B, W), BF16),
            pltpu.VMEM((P2, W), BF16),
            pltpu.VMEM((B, P2), BF16),
            dma((S,)), dma((S,)), dma((S,)), dma((S,)), dma((1,)), dma((1,)),
            dma((2, 8, SUBS)), dma((2, 8, SUBS)), dma((2, S)), dma((2, S)),
            dma((2 * Z,)), dma((1,)), dma((2, 8, SUBS)), dma((2, 8, SUBS)),
            dma((Z,)), dma((Z,)), dma((S,)), dma((1,)),
        ],
        compiler_params=pltpu.CompilerParams(
            collective_id=0, has_side_effects=True, vmem_limit_bytes=48 << 20
        ),
        name="exchange",
    )(a, panel, m, parent_front, parent_inverse, parent_pivots)


def solution(mesh):
    in_specs = (
        P("helpers", "subtree"),
        P("helpers", "subtree"),
        P("subtree", None, None),
        P(),
        P("subtree", None),
        P("subtree", None),
        P("subtree"),
        P("subtree"),
        P(),
    )
    return jax.shard_map(
        local, mesh=mesh, in_specs=in_specs, out_specs=P("helpers", "subtree"), check_vma=False
    )
```

time: 525 us -> 133 us (0.25)
  the two profiles are of different devices: /device:TPU:7 before, /device:TPU:29 now
where the time goes in v1:
time: 133 us
  Pallas kernels  126 us (95%)
  local copies, waits for them, and re-layouts  4.47 us (3%)
  between operations  1.99 us (1%)
    pallas_call x1, Pallas kernels, local(): pl.pallas_call(exchange_kernel, out_shape=jax.ShapeDtypeStruct((B, W), BF...  114 us
    pallas_call x1, Pallas kernels, local(): pl.pallas_call(permute_kernel, out_shape=(jax.ShapeDtypeStruct((S, B, W),...  12.9 us
    unnamed x13, local copies, waits for them, and re-layouts  4.47 us

profile of v1, /device:TPU:29, one launch (start us, length us, event | category | flops | bytes accessed | tf_op | source)
XLA Modules:
  0.0 132.9 jit_solution(3291162083237936700)
XLA Ops:
  1.9 0.0 copy-start
  2.0 1.6 %copy-done = bf16[128,8192]{1,0:T(8,128)(2,1)S(1)} copy-done((bf16[128,8192]{1,0:T(8,128)(2,1)S(1)}, bf16[128,8192]{1,0:T(8,128)(2,1)}, u32[]{:S(2)}) %copy-start) | copy-done | bytes 2097176
  3.5 0.0 copy-start.3
  3.5 0.8 copy-done.3
  4.3 0.0 copy-start.4
  4.3 0.8 copy-done.4
  5.1 0.0 copy-start.5
  5.1 0.7 copy-done.5
  5.7 0.0 copy-start.1
  5.7 0.0 copy-start.2
  5.7 12.9 %permute.1 = (bf16[8,128,1024]{2,1,0:T(8,128)(2,1)S(1)}, bf16[2,16,8,16,256]{4,3,2,1,0:T(8,128)(2,1)S(1)}, bf16[128,128]{1,0:T(8,128)(2,1)S(1)}) custom-call(s32[1]{0:T(128)} %bitcast.h_ref, s32[1,64]{1,0:T(1,128)S(1)} %copy-done.5, s32[1]{0:T(128)S(6)} %copy.11.order_ref, s32[1]{0:T(128)S(6)} %copy.12.pivots_ref, s32[1,8192]{1,0:T(1,128)S(1)} %copy-done.3, ...), custom_call_target="tpu_custom_call" | custom-call | tf_op jit(solution)/shard_map/permute/pallas_call | solution.py:285
  18.6 0.0 copy-done.1
  18.6 0.0 copy-done.2
  18.6 113.6 %exchange.1 = bf16[128,1024]{1,0:T(8,128)(2,1)S(1)} custom-call(bf16[8,128,1024]{2,1,0:T(8,128)(2,1)S(1)} %get-tuple-element.8.a_ref, bf16[2,16,8,16,256]{4,3,2,1,0:T(8,128)(2,1)S(1)} %get-tuple-element.9.panel_ref, bf16[128,128]{1,0:T(8,128)(2,1)S(1)} %get-tuple-element.10.m_ref, bf16[128,1024]{1,0:T(8,128)(2,1)S(1)} %copy-done.1, ...), custom_call_target="tpu_custom_call" | custom-call | tf_op jit(solution)/shard_map/exchange/pallas_call | solution.py:298
  132.2 0.7 copy.14
Async XLA Ops:
  1.9 1.6 %copy-start = (bf16[128,8192]{1,0:T(8,128)(2,1)S(1)}, bf16[128,8192]{1,0:T(8,128)(2,1)}, u32[]{:S(2)}) copy-start(bf16[128,8192]{1,0:T(8,128)(2,1)} %front_ref.1) | copy-start | bytes 6291460
  3.5 0.8 copy-start.3
  4.3 0.8 copy-start.4
  5.1 0.7 copy-start.5
  5.7 12.9 %copy-start.1 = (bf16[128,1024]{1,0:T(8,128)(2,1)S(1)}, bf16[128,1024]{1,0:T(8,128)(2,1)}, u32[]{:S(2)}) copy-start(bf16[128,1024]{1,0:T(8,128)(2,1)} %parent_ref.1) | copy-start | bytes 786436
  5.7 12.9 %copy-start.2 = (bf16[256,256]{1,0:T(8,128)(2,1)S(1)}, bf16[256,256]{1,0:T(8,128)(2,1)}, u32[]{:S(2)}) copy-start(bf16[256,256]{1,0:T(8,128)(2,1)} %pinv_ref.1) | copy-start | bytes 393220

commit v2 on v1

v2 whole, which is shorter than its diff:
```python
import jax
import jax.numpy as jnp
from jax import lax
from jax.experimental import pallas as pl
from jax.experimental.pallas import tpu as pltpu
from jax.sharding import PartitionSpec as P

MESH = pl.DeviceIdType.MESH
BF16 = jnp.bfloat16
F32 = jnp.float32
B = 128
S = 8
Z = 16
W = 1024
P2 = 256
T = 16
CUTS = ((0, 4), (4, 5))


def prepare_kernel(
    h_ref, plan_hbm, order_hbm, pivots_hbm, front_hbm, map_hbm, inv_hbm, blocks_ref, panel_ref, place_ref, m_ref,
    plan, order_ref, pivots_ref, front, place_of, inv, in_s,
):
    copies = []
    for n, (src, dst) in enumerate((
        (plan_hbm, plan), (front_hbm, front), (order_hbm, order_ref), (pivots_hbm, pivots_ref), (map_hbm, place_of),
        (inv_hbm, inv),
    )):
        copies.append(pltpu.make_async_copy(src, dst, in_s.at[n]))
        copies[-1].start()
    for copy in copies:
        copy.wait()
    h = h_ref[0]
    order = order_ref[0]
    root = plan[0, h] == 0
    lanes = lax.broadcasted_iota(jnp.int32, (1, B), 1)

    @pl.loop(0, S)
    def _(c):
        for i in range(W // B):
            j = c * (W // B) + i
            block = plan[0, j]
            columns = pl.ds(pl.multiple_of(block * B, B), B)
            index = block * B + lanes
            place = jnp.where((index >= B) & (index < order), place_of[:, columns] - j * B, -1)
            place_ref[pl.ds(j, 1), :] = place
            x = front[:, columns]
            blocks_ref[c, :, i * B : (i + 1) * B] = x
            x = jnp.where(root, x, jnp.zeros_like(x))
            for r in range(B // T):
                p = r * 4 + i // 2
                panel_ref[p // Z, p % Z, c, :, (i % 2) * B : (i % 2 + 1) * B] = x[r * T : (r + 1) * T]

    rows = lax.broadcasted_iota(jnp.int32, (B, B), 0)
    own = jnp.where(rows == place_ref[pl.ds(h, 1), :], 1.0, 0.0).astype(BF16)
    m = jnp.dot(front[:, :B], inv[0], preferred_element_type=F32)
    m = jnp.where(lanes < pivots_ref[0], m, 0.0).astype(BF16)
    m_ref[...] = jnp.dot(own, m, preferred_element_type=F32).astype(BF16)


def kernel(
    blocks_ref, panel, place_ref, m_out, parent, pinv, pp_ref, o_ref,
    sib, part, up_buf, dn_buf, piece, spread, select, a_out, a_in, m_in, raw,
    lhs, rhs, mg, mb, bc, asm, prow, pm,
    a_s, a_r, m_s, m_r, sib_s, sib_r, rs_s, rs_r, sp_s, sp_r, sc_s, sc_r, bc_s, bc_r, ag_s, ag_r,
    fw_s, fw_r, bf_s, bf_r, pm_s, pm_r,
):
    h = lax.axis_index("helpers")
    s = lax.axis_index("subtree")
    y, z, k = h // (2 * Z), (h // 2) % Z, h % 2

    def at(y, z, k):
        return y * (2 * Z) + z * 2 + k

    def along(dz):
        return (at(y, (z + Z + dz) % Z, k), s)

    up, dn = along(1), along(-1)
    sibling = (at(y, z, 1 - k), s)
    plane = [(dy, d) for dy in range(2) for d in range(S) if dy or d]
    first = jnp.logical_and(y == 0, z == 0)

    def plane_peer(dy, d):
        return (at((y + dy) % 2, z, k), (s + d) % S)

    def remote(src, dst, send, recv, device):
        return pltpu.make_async_remote_copy(
            src_ref=src, dst_ref=dst, send_sem=send, recv_sem=recv, device_id=device, device_id_type=MESH
        )

    sent = []

    def start(*args):
        copy = remote(*args)
        copy.start()
        sent.append(copy)
        return copy

    barrier = pltpu.get_barrier_semaphore()
    peers = [up, dn, sibling] + [plane_peer(*e) for e in plane]
    for peer in peers:
        pl.semaphore_signal(barrier, inc=1, device_id=peer, device_id_type=MESH)
    pl.semaphore_wait(barrier, len(peers))
    cross = start(panel.at[1 - k], sib, sib_s.at[0], sib_r.at[0], sibling)

    rows_iota = lax.broadcasted_iota(jnp.int32, (B, B), 0)

    def selector(j):
        return jnp.where(rows_iota == place_ref[pl.ds(j, 1), :], 1.0, 0.0).astype(BF16)

    own = selector(h)
    m_copies = [start(m_out, m_in.at[d], m_s.at[d], m_r.at[d], (h, (s + d) % S)) for d in range(1, S)]

    cross.wait_recv()

    @pl.loop(0, Z)
    def _(j):
        part[j, :S] = panel[k, j] + sib[j]

    for j in range(Z):
        tile = m_out[(j // 2) * T : (j // 2 + 1) * T]
        tile = jnp.where(first, tile, jnp.zeros_like(tile))
        part[j, S, :, :B] = tile
        part[j, S, :, B:] = tile

    a_copies = []

    def permute(d):
        c = (s + d) % S
        blocks = []
        for i in range(W // B):
            j = c * (W // B) + i
            x = blocks_ref[c, :, i * B : (i + 1) * B]
            x = lax.dot_general(x, selector(j), (((1,), (1,)), ((), ())), preferred_element_type=F32)
            blocks.append(x.astype(BF16))
        x = jnp.concatenate(blocks, axis=1)
        a_out[d] = jnp.dot(own, x, preferred_element_type=F32).astype(BF16)
        if d:
            a_copies.append(start(a_out.at[d], a_in.at[d], a_s.at[d], a_r.at[d], (h, c)))

    def selectors():
        for n in range(2 * S):
            select[n] = selector((n // 2) * (W // B) + (z % 4) * 2 + n % 2)

    rs = {}
    for t in range(8):
        for i, (low, count) in enumerate(CUTS):
            cut = pl.ds(low, count)
            for way, (buf, peer) in enumerate(((up_buf, up), (dn_buf, dn))):
                if way == 1 and t == 7:
                    continue
                j = (z + 8 - t) % Z if way == 0 else (z + Z - 7 + t) % Z
                if t == 0:
                    src = part.at[j, cut]
                else:
                    rs[way, i].wait_recv()
                    buf[t - 1, cut] = buf[t - 1, cut] + part[j, cut]
                    src = buf.at[t - 1, cut]
                rs[way, i] = start(src, buf.at[t, cut], rs_s.at[way, t, i], rs_r.at[way, t, i], peer)
        if t < 4:
            permute((2 * t + 1) % S)
            permute((2 * t + 2) % S)
        if t == 4:
            selectors()
        if t == 5:
            for copy in m_copies:
                copy.wait_recv()
            lhs[:B, pl.ds(pl.multiple_of(s * B, B), B)] = m_out[...]
            for d in range(1, S):
                lhs[:B, pl.ds(pl.multiple_of((s + S - d) % S * B, B), B)] = m_in[d]

    for i in range(len(CUTS)):
        rs[0, i].wait_recv()
        rs[1, i].wait_recv()

    tile = part[z, S] + up_buf[7, S] + dn_buf[6, S]
    for c in range(S):
        x = part[z, c] + up_buf[7, c] + dn_buf[6, c]
        for i in range(2):
            half = lax.dot_general(
                x[:, i * B : (i + 1) * B], select[2 * c + i], (((1,), (1,)), ((), ())), preferred_element_type=F32
            )
            piece[c, 0, :, i * B : (i + 1) * B] = half.astype(BF16)
        piece[c, 1] = tile
    spreads = [
        start(piece.at[(s + d) % S], spread.at[dy, d], sp_s.at[dy, d], sp_r.at[dy, d], plane_peer(dy, d))
        for dy, d in plane
    ]
    for copy in spreads:
        copy.wait_recv()
    quarter, high = z % 4, k * 4 + z // 4
    for d in range(S):
        source = (s + S - d) % S
        mine = piece[s] if d == 0 else spread[0, d]
        mine = mine + spread[1, d]
        rhs[quarter, source, high] = mine[0]
        spread[0, d] = mine

    for u in range(4):
        d = (s + S - (z % 2) * 4 - u) % S
        mg[k, z, (u // 2) * T : (u // 2 + 1) * T, (u % 2) * B : (u % 2 + 1) * B] = spread[0, d, 1, :, :B]

    ag, forwards, levels = {}, [], []

    def parts(j):
        return (
            rhs.at[j % 4, pl.ds(0, 4), k * 4 + j // 4],
            rhs.at[j % 4, pl.ds(4, 4), k * 4 + j // 4],
            mg.at[k, j],
        )

    def forward(n, j):
        for i, ref in enumerate((rhs.at[j % 4, :, k * 4 + j // 4], mg.at[k, j])):
            forwards.append(start(ref, ref, fw_s.at[n, i], fw_r.at[n, i], sibling))

    def scatter(e):
        j = e % Z
        return remote(mb.at[j], bc.at[k, j % 4, j // 4], sc_s.at[e], sc_r.at[0], (at(e // Z, j, k), s))

    def sums():
        for copy in a_copies:
            copy.wait_recv()

        @pl.loop(0, B // T)
        def _(g):
            rows = pl.ds(pl.multiple_of(g * T, T), T)
            total = parent[rows].astype(F32) + a_out[0, rows].astype(F32)
            for d in range(1, S):
                total += a_in[d, rows].astype(F32)
            raw[rows] = total
            rounded = total.astype(BF16)
            for q in range(4):
                mb[g * 2 + q // 2, (q % 2) * T : (q % 2 + 1) * T] = rounded[:, q * P2 : (q + 1) * P2]

        @pl.when(first)
        def _():
            for e in range(1, 2 * Z):
                scatter(e).start()
            bc[k, 0, 0] = mb[0]

    def level_a():
        @pl.when(jnp.logical_not(first))
        def _():
            remote(mb.at[0], bc.at[k, z % 4, z // 4], sc_s.at[0], sc_r.at[0], sibling).wait_recv()

        ref = bc.at[k, z % 4, z // 4]
        for n, dz in enumerate((4, 8, 12)):
            levels.append(start(ref, ref, bc_s.at[n], bc_r.at[n], along(dz)))

    def level_b():
        for copy in levels:
            copy.wait_recv()
        del levels[:]
        ref = bc.at[k, z % 4]
        for n, dz in enumerate((1, -1, 2)):
            levels.append(start(ref, ref, bc_s.at[3 + n], bc_r.at[3 + n], along(dz)))

    for t in range(9):
        for i in range(3):
            for way, peer in ((0, up), (1, dn)):
                j = (z + Z - t) % Z if way == 0 else (z + t) % Z
                if t > 0 and not (way == 1 and t == 8):
                    ag[way, i].wait_recv()
                if t < 8 - way:
                    ref = parts(j)[i]
                    ag[way, i] = start(ref, ref, ag_s.at[way, t, i], ag_r.at[way, t, i], peer)
        forward(t, (z + Z - t) % Z)
        if 0 < t < 8:
            forward(8 + t, (z + t) % Z)
        if t == 0:
            sums()
        if t == 4:
            level_a()
        if t == 7:
            level_b()
    for copy in levels:
        copy.wait_recv()
    last = start(bc.at[k], bc.at[k], bf_s.at[0], bf_r.at[0], sibling)
    for copy in forwards + [last]:
        copy.wait_recv()

    for p in range(2 * Z):
        for u in range(4):
            top = B + (p // Z) * B + (p % Z) // 2 * T
            left = ((p % 2) * 4 + u) * B
            lhs[top : top + T, left : left + B] = mg[
                p // Z, p % Z, (u // 2) * T : (u // 2 + 1) * T, (u % 2) * B : (u % 2 + 1) * B
            ]

    def assemble(q):
        cols = slice(q * P2, (q + 1) * P2)
        update = jnp.dot(lhs[...], rhs[q].reshape(S * B, P2), preferred_element_type=F32)
        asm[:, cols] = (raw[:, cols] - update[:B]).astype(BF16)
        for p in range(Z):
            j = (p % 8) * 2 + q // 2
            base = bc[p // 8, j % 4, j // 4, (q % 2) * T : (q % 2 + 1) * T].astype(F32)
            prow[p * T : (p + 1) * T, cols] = (base - update[B + p * T : B + (p + 1) * T]).astype(BF16)

    assemble(0)

    def pm_copy(d):
        return remote(pm, pm, pm_s.at[d], pm_r.at[0], (h, (s + d) % S))

    @pl.when(s == 0)
    def _():
        m = jnp.dot(asm[:, :P2], pinv[...], preferred_element_type=F32)
        lanes = lax.broadcasted_iota(jnp.int32, (1, P2), 1)
        pm[...] = jnp.where(lanes < pp_ref[0], m, 0.0).astype(BF16)
        for d in range(1, S):
            pm_copy(d).start()

    for q in range(1, 4):
        assemble(q)

    @pl.when(s != 0)
    def _():
        pm_copy(1).wait_recv()

    for q in range(4):
        cols = slice(q * P2, (q + 1) * P2)
        update = jnp.dot(pm[...], prow[:, cols], preferred_element_type=F32)
        o_ref[:, cols] = (asm[:, cols].astype(F32) - update).astype(BF16)

    for copy in sent:
        copy.wait_send()

    @pl.when(first)
    def _():
        for e in range(1, 2 * Z):
            scatter(e).wait_send()

    @pl.when(s == 0)
    def _():
        for d in range(1, S):
            pm_copy(d).wait_send()


def local(
    child_fronts,
    parent_front,
    child_inverse,
    parent_inverse,
    helper_plan,
    child_map,
    child_orders,
    child_pivots,
    parent_pivots,
):
    vmem, smem, dma = pltpu.VMEM, pltpu.SMEM, pltpu.SemaphoreType.DMA
    h = jnp.reshape(lax.axis_index("helpers"), (1,)).astype(jnp.int32)
    in_vmem = pl.BlockSpec(memory_space=vmem)
    in_smem = pl.BlockSpec(memory_space=smem)
    blocks, panel, place, m = pl.pallas_call(
        prepare_kernel,
        out_shape=(
            jax.ShapeDtypeStruct((S, B, W), BF16),
            jax.ShapeDtypeStruct((2, Z, S, T, P2), BF16),
            jax.ShapeDtypeStruct((64, B), jnp.int32),
            jax.ShapeDtypeStruct((B, B), BF16),
        ),
        in_specs=[in_smem] + [pl.BlockSpec(memory_space=pl.ANY)] * 6,
        out_specs=(in_vmem,) * 4,
        scratch_shapes=[
            smem((1, 64), jnp.int32),
            smem((1,), jnp.int32),
            smem((1,), jnp.int32),
            vmem((B, S * W), BF16),
            vmem((1, S * W), jnp.int32),
            vmem((1, B, B), BF16),
            dma((6,)),
        ],
        compiler_params=pltpu.CompilerParams(vmem_limit_bytes=24 << 20),
        name="prepare",
    )(h, helper_plan, child_orders, child_pivots, child_fronts, child_map, child_inverse)
    return pl.pallas_call(
        kernel,
        out_shape=jax.ShapeDtypeStruct((B, W), BF16),
        in_specs=[in_vmem] * 6 + [in_smem],
        out_specs=in_vmem,
        scratch_shapes=[
            vmem((Z, S, T, P2), BF16),
            vmem((Z, S + 1, T, P2), BF16),
            vmem((8, S + 1, T, P2), BF16),
            vmem((7, S + 1, T, P2), BF16),
            vmem((S, 2, T, P2), BF16),
            vmem((2, S, 2, T, P2), BF16),
            vmem((2 * S, B, B), BF16),
            vmem((S, B, W), BF16),
            vmem((S, B, W), BF16),
            vmem((S, B, B), BF16),
            vmem((B, W), F32),
            vmem((B + P2, S * B), BF16),
            vmem((4, S, B // T, T, P2), BF16),
            vmem((2, Z, 2 * T, P2), BF16),
            vmem((Z, 2 * T, P2), BF16),
            vmem((2, 4, 4, 2 * T, P2), BF16),
            vmem((B, W), BF16),
            vmem((P2, W), BF16),
            vmem((B, P2), BF16),
            dma((S,)), dma((S,)), dma((S,)), dma((S,)), dma((1,)), dma((1,)),
            dma((2, 8, 2)), dma((2, 8, 2)), dma((2, S)), dma((2, S)),
            dma((2 * Z,)), dma((1,)), dma((6,)), dma((6,)), dma((2, 8, 3)), dma((2, 8, 3)),
            dma((Z, 2)), dma((Z, 2)), dma((1,)), dma((1,)), dma((S,)), dma((1,)),
        ],
        compiler_params=pltpu.CompilerParams(
            collective_id=0, has_side_effects=True, vmem_limit_bytes=40 << 20
        ),
        name="exchange",
    )(blocks, panel, place, m, parent_front, parent_inverse, parent_pivots)


def solution(mesh):
    in_specs = (
        P("helpers", "subtree"),
        P("helpers", "subtree"),
        P("subtree", None, None),
        P(),
        P("subtree", None),
        P("subtree", None),
        P("subtree"),
        P("subtree"),
        P(),
    )
    return jax.shard_map(
        local, mesh=mesh, in_specs=in_specs, out_specs=P("helpers", "subtree"), check_vma=False
    )
```

time: 133 us -> 108 us (0.81)
  the two profiles are of different devices: /device:TPU:29 before, /device:TPU:21 now
where the time goes in v2:
time: 108 us; the launch traced here: 107 us
  Pallas kernels  101 us (94%)
  local copies, waits for them, and re-layouts  4.47 us (4%)
  between operations  1.99 us (2%)
    pallas_call x1, Pallas kernels, local(): pl.pallas_call(kernel, out_shape=jax.ShapeDtypeStruct((B, W), BF16), in_s...  98.9 us
    unnamed x13, local copies, waits for them, and re-layouts  4.47 us

profile of v2, /device:TPU:21, one launch (start us, length us, event | category | flops | bytes accessed | tf_op | source)
XLA Modules:
  0.0 107.2 jit_solution(530221531832548849)
XLA Ops:
  1.9 0.0 copy-start
  2.0 1.6 %copy-done = bf16[128,8192]{1,0:T(8,128)(2,1)S(1)} copy-done((bf16[128,8192]{1,0:T(8,128)(2,1)S(1)}, bf16[128,8192]{1,0:T(8,128)(2,1)}, u32[]{:S(2)}) %copy-start) | copy-done | bytes 2097176
  3.5 0.0 copy-start.3
  3.5 0.8 copy-done.3
  4.3 0.0 copy-start.4
  4.3 0.8 copy-done.4
  5.1 0.0 copy-start.5
  5.1 0.7 copy-done.5
  5.7 0.0 copy-start.1
  5.7 0.0 copy-start.2
  5.7 1.9 %prepare.1 = (bf16[8,128,1024]{2,1,0:T(8,128)(2,1)S(1)}, bf16[2,16,8,16,256]{4,3,2,1,0:T(8,128)(2,1)S(1)}, s32[64,128]{1,0:T(8,128)S(1)}, bf16[128,128]{1,0:T(8,128)(2,1)S(1)}) custom-call(s32[1]{0:T(128)} %bitcast.h_ref, s32[1,64]{1,0:T(1,128)S(1)} %copy-done.5, s32[1]{0:T(128)S(6)} %copy.11.order_hbm, s32[1]{0:T(128)S(6)} %copy.12.pivots_hbm, ...), custom_call_target="tpu_custom_call" | custom-call | tf_op jit(solution)/shard_map/prepare/pallas_call | solution.py:353
  7.6 0.0 copy-done.1
  7.6 0.0 copy-done.2
  7.6 98.9 %exchange.1 = bf16[128,1024]{1,0:T(8,128)(2,1)S(1)} custom-call(bf16[8,128,1024]{2,1,0:T(8,128)(2,1)S(1)} %get-tuple-element.9.blocks_ref, bf16[2,16,8,16,256]{4,3,2,1,0:T(8,128)(2,1)S(1)} %get-tuple-element.10.panel, s32[64,128]{1,0:T(8,128)S(1)} %get-tuple-element.11.place_ref, bf16[128,128]{1,0:T(8,128)(2,1)S(1)} %get-tuple-element.12.m_out, ...), custom_call_target="tpu_custom_call" | custom-call | tf_op jit(solution)/shard_map/exchange/pallas_call | solution.py:375
  106.5 0.7 copy.14
Async XLA Ops:
  1.9 1.6 %copy-start = (bf16[128,8192]{1,0:T(8,128)(2,1)S(1)}, bf16[128,8192]{1,0:T(8,128)(2,1)}, u32[]{:S(2)}) copy-start(bf16[128,8192]{1,0:T(8,128)(2,1)} %front_hbm.1) | copy-start | bytes 6291460
  3.5 0.8 copy-start.3
  4.3 0.8 copy-start.4
  5.1 0.7 copy-start.5
  5.7 1.9 %copy-start.1 = (bf16[128,1024]{1,0:T(8,128)(2,1)S(1)}, bf16[128,1024]{1,0:T(8,128)(2,1)}, u32[]{:S(2)}) copy-start(bf16[128,1024]{1,0:T(8,128)(2,1)} %parent.1) | copy-start | bytes 786436
  5.7 1.9 %copy-start.2 = (bf16[256,256]{1,0:T(8,128)(2,1)S(1)}, bf16[256,256]{1,0:T(8,128)(2,1)}, u32[]{:S(2)}) copy-start(bf16[256,256]{1,0:T(8,128)(2,1)} %pinv.1) | copy-start | bytes 393220

commit v3 on v2

--- a/solution.py
+++ b/solution.py
@@ -157,9 +157,7 @@
                     buf[t - 1, cut] = buf[t - 1, cut] + part[j, cut]
                     src = buf.at[t - 1, cut]
                 rs[way, i] = start(src, buf.at[t, cut], rs_s.at[way, t, i], rs_r.at[way, t, i], peer)
-        if t < 4:
-            permute((2 * t + 1) % S)
-            permute((2 * t + 2) % S)
+        permute((2, 6, 4, 5, 3, 1, 7, 0)[t])
         if t == 4:
             selectors()
         if t == 5:
@@ -269,9 +267,9 @@
             forward(8 + t, (z + t) % Z)
         if t == 0:
             sums()
-        if t == 4:
+        if t == 3:
             level_a()
-        if t == 7:
+        if t == 6:
             level_b()
     for copy in levels:
         copy.wait_recv()

time: 108 us -> 100 us (0.926)
  Pallas kernels: 101 us -> 93.6 us
    pallas_call x1, Pallas kernels: 98.9 us -> 91.7 us  [local(): pl.pallas_call(kernel, out_shape=jax.ShapeDtypeStruct((B, W), BF16), in_s...]
where the time goes in v3:
time: 100 us
  Pallas kernels  93.6 us (94%)
  local copies, waits for them, and re-layouts  4.47 us (4%)
  between operations  1.99 us (2%)
    pallas_call x1, Pallas kernels, local(): pl.pallas_call(kernel, out_shape=jax.ShapeDtypeStruct((B, W), BF16), in_s...  91.7 us
    unnamed x13, local copies, waits for them, and re-layouts  4.47 us

profile of v3, /device:TPU:21, one launch (start us, length us, event | category | flops | bytes accessed | tf_op | source)
XLA Modules:
  0.0 100.0 jit_solution(376748015098010045)
XLA Ops:
  1.9 0.0 copy-start
  2.0 1.6 %copy-done = bf16[128,8192]{1,0:T(8,128)(2,1)S(1)} copy-done((bf16[128,8192]{1,0:T(8,128)(2,1)S(1)}, bf16[128,8192]{1,0:T(8,128)(2,1)}, u32[]{:S(2)}) %copy-start) | copy-done | bytes 2097176
  3.5 0.0 copy-start.3
  3.5 0.8 copy-done.3
  4.3 0.0 copy-start.4
  4.3 0.8 copy-done.4
  5.1 0.0 copy-start.5
  5.1 0.7 copy-done.5
  5.7 0.0 copy-start.1
  5.7 0.0 copy-start.2
  5.7 1.9 %prepare.1 = (bf16[8,128,1024]{2,1,0:T(8,128)(2,1)S(1)}, bf16[2,16,8,16,256]{4,3,2,1,0:T(8,128)(2,1)S(1)}, s32[64,128]{1,0:T(8,128)S(1)}, bf16[128,128]{1,0:T(8,128)(2,1)S(1)}) custom-call(s32[1]{0:T(128)} %bitcast.h_ref, s32[1,64]{1,0:T(1,128)S(1)} %copy-done.5, s32[1]{0:T(128)S(6)} %copy.11.order_hbm, s32[1]{0:T(128)S(6)} %copy.12.pivots_hbm, ...), custom_call_target="tpu_custom_call" | custom-call | tf_op jit(solution)/shard_map/prepare/pallas_call | solution.py:351
  7.6 0.0 copy-done.1
  7.6 0.0 copy-done.2
  7.6 91.7 %exchange.1 = bf16[128,1024]{1,0:T(8,128)(2,1)S(1)} custom-call(bf16[8,128,1024]{2,1,0:T(8,128)(2,1)S(1)} %get-tuple-element.9.blocks_ref, bf16[2,16,8,16,256]{4,3,2,1,0:T(8,128)(2,1)S(1)} %get-tuple-element.10.panel, s32[64,128]{1,0:T(8,128)S(1)} %get-tuple-element.11.place_ref, bf16[128,128]{1,0:T(8,128)(2,1)S(1)} %get-tuple-element.12.m_out, ...), custom_call_target="tpu_custom_call" | custom-call | tf_op jit(solution)/shard_map/exchange/pallas_call | solution.py:373
  99.3 0.7 copy.14
Async XLA Ops:
  1.9 1.6 %copy-start = (bf16[128,8192]{1,0:T(8,128)(2,1)S(1)}, bf16[128,8192]{1,0:T(8,128)(2,1)}, u32[]{:S(2)}) copy-start(bf16[128,8192]{1,0:T(8,128)(2,1)} %front_hbm.1) | copy-start | bytes 6291460
  3.5 0.8 copy-start.3
  4.3 0.8 copy-start.4
  5.1 0.7 copy-start.5
  5.7 1.9 %copy-start.1 = (bf16[128,1024]{1,0:T(8,128)(2,1)S(1)}, bf16[128,1024]{1,0:T(8,128)(2,1)}, u32[]{:S(2)}) copy-start(bf16[128,1024]{1,0:T(8,128)(2,1)} %parent.1) | copy-start | bytes 786436
  5.7 1.9 %copy-start.2 = (bf16[256,256]{1,0:T(8,128)(2,1)S(1)}, bf16[256,256]{1,0:T(8,128)(2,1)}, u32[]{:S(2)}) copy-start(bf16[256,256]{1,0:T(8,128)(2,1)} %pinv.1) | copy-start | bytes 393220

commit v4 on v3

--- a/solution.py
+++ b/solution.py
@@ -14,17 +14,16 @@
 W = 1024
 P2 = 256
 T = 16
-CUTS = ((0, 4), (4, 5))
+CUTS = ((0, 9),)
 
 
 def prepare_kernel(
-    h_ref, plan_hbm, order_hbm, pivots_hbm, front_hbm, map_hbm, inv_hbm, blocks_ref, panel_ref, place_ref, m_ref,
-    plan, order_ref, pivots_ref, front, place_of, inv, in_s,
+    h_ref, plan_hbm, order_hbm, front_hbm, map_hbm, blocks_ref, panel_ref, place_ref, lead_ref,
+    plan, order_ref, front, place_of, in_s,
 ):
     copies = []
     for n, (src, dst) in enumerate((
-        (plan_hbm, plan), (front_hbm, front), (order_hbm, order_ref), (pivots_hbm, pivots_ref), (map_hbm, place_of),
-        (inv_hbm, inv),
+        (plan_hbm, plan), (front_hbm, front), (order_hbm, order_ref), (map_hbm, place_of),
     )):
         copies.append(pltpu.make_async_copy(src, dst, in_s.at[n]))
         copies[-1].start()
@@ -51,16 +50,12 @@
                 p = r * 4 + i // 2
                 panel_ref[p // Z, p % Z, c, :, (i % 2) * B : (i % 2 + 1) * B] = x[r * T : (r + 1) * T]
 
-    rows = lax.broadcasted_iota(jnp.int32, (B, B), 0)
-    own = jnp.where(rows == place_ref[pl.ds(h, 1), :], 1.0, 0.0).astype(BF16)
-    m = jnp.dot(front[:, :B], inv[0], preferred_element_type=F32)
-    m = jnp.where(lanes < pivots_ref[0], m, 0.0).astype(BF16)
-    m_ref[...] = jnp.dot(own, m, preferred_element_type=F32).astype(BF16)
+    lead_ref[...] = front[:, :B]
 
 
 def kernel(
-    blocks_ref, panel, place_ref, m_out, parent, pinv, pp_ref, o_ref,
-    sib, part, up_buf, dn_buf, piece, spread, select, a_out, a_in, m_in, raw,
+    blocks_ref, panel, place_ref, lead, inv, parent, pinv, pivots_ref, pp_ref, o_ref,
+    m_out, sib, part, up_buf, dn_buf, piece, spread, select, a_out, a_in, m_in, raw,
     lhs, rhs, mg, mb, bc, asm, prow, pm,
     a_s, a_r, m_s, m_r, sib_s, sib_r, rs_s, rs_r, sp_s, sp_r, sc_s, sc_r, bc_s, bc_r, ag_s, ag_r,
     fw_s, fw_r, bf_s, bf_r, pm_s, pm_r,
@@ -109,6 +104,9 @@
         return jnp.where(rows_iota == place_ref[pl.ds(j, 1), :], 1.0, 0.0).astype(BF16)
 
     own = selector(h)
+    m = jnp.dot(lead[...], inv[0], preferred_element_type=F32)
+    m = jnp.where(lax.broadcasted_iota(jnp.int32, (1, B), 1) < pivots_ref[0], m, 0.0).astype(BF16)
+    m_out[...] = jnp.dot(own, m, preferred_element_type=F32).astype(BF16)
     m_copies = [start(m_out, m_in.at[d], m_s.at[d], m_r.at[d], (h, (s + d) % S)) for d in range(1, S)]
 
     cross.wait_recv()
@@ -348,7 +346,7 @@
     h = jnp.reshape(lax.axis_index("helpers"), (1,)).astype(jnp.int32)
     in_vmem = pl.BlockSpec(memory_space=vmem)
     in_smem = pl.BlockSpec(memory_space=smem)
-    blocks, panel, place, m = pl.pallas_call(
+    blocks, panel, place, lead = pl.pallas_call(
         prepare_kernel,
         out_shape=(
             jax.ShapeDtypeStruct((S, B, W), BF16),
@@ -356,26 +354,25 @@
             jax.ShapeDtypeStruct((64, B), jnp.int32),
             jax.ShapeDtypeStruct((B, B), BF16),
         ),
-        in_specs=[in_smem] + [pl.BlockSpec(memory_space=pl.ANY)] * 6,
+        in_specs=[in_smem] + [pl.BlockSpec(memory_space=pl.ANY)] * 4,
         out_specs=(in_vmem,) * 4,
         scratch_shapes=[
             smem((1, 64), jnp.int32),
             smem((1,), jnp.int32),
-            smem((1,), jnp.int32),
             vmem((B, S * W), BF16),
             vmem((1, S * W), jnp.int32),
-            vmem((1, B, B), BF16),
-            dma((6,)),
+            dma((4,)),
         ],
         compiler_params=pltpu.CompilerParams(vmem_limit_bytes=24 << 20),
         name="prepare",
-    )(h, helper_plan, child_orders, child_pivots, child_fronts, child_map, child_inverse)
+    )(h, helper_plan, child_orders, child_fronts, child_map)
     return pl.pallas_call(
         kernel,
         out_shape=jax.ShapeDtypeStruct((B, W), BF16),
-        in_specs=[in_vmem] * 6 + [in_smem],
+        in_specs=[in_vmem] * 7 + [in_smem] * 2,
         out_specs=in_vmem,
         scratch_shapes=[
+            vmem((B, B), BF16),
             vmem((Z, S, T, P2), BF16),
             vmem((Z, S + 1, T, P2), BF16),
             vmem((8, S + 1, T, P2), BF16),
@@ -404,7 +401,9 @@
             collective_id=0, has_side_effects=True, vmem_limit_bytes=40 << 20
         ),
         name="exchange",
-    )(blocks, panel, place, m, parent_front, parent_inverse, parent_pivots)
+    )(
+        blocks, panel, place, lead, child_inverse, parent_front, parent_inverse, child_pivots, parent_pivots
+    )
 
 
 def solution(mesh):

time: 100 us -> 101 us (1.010)
  Pallas kernels: 93.6 us -> 95.5 us
    pallas_call x1, Pallas kernels: 91.7 us -> 93.9 us  [local(): pl.pallas_call(kernel, out_shape=jax.ShapeDtypeStruct((B, W), BF16), in_s...]
where the time goes in v4:
time: 101 us
  Pallas kernels  95.5 us (95%)
  local copies, waits for them, and re-layouts  3.71 us (4%)
  between operations  1.99 us (2%)
    pallas_call x1, Pallas kernels, local(): pl.pallas_call(kernel, out_shape=jax.ShapeDtypeStruct((B, W), BF16), in_s...  93.9 us
    unnamed x13, local copies, waits for them, and re-layouts  3.71 us

profile of v4, /device:TPU:21, one launch (start us, length us, event | category | flops | bytes accessed | tf_op | source)
XLA Modules:
  0.0 101.2 jit_solution(1620657584948220471)
XLA Ops:
  1.9 0.0 copy-start
  2.0 1.6 %copy-done = bf16[128,8192]{1,0:T(8,128)(2,1)S(1)} copy-done((bf16[128,8192]{1,0:T(8,128)(2,1)S(1)}, bf16[128,8192]{1,0:T(8,128)(2,1)}, u32[]{:S(2)}) %copy-start) | copy-done | bytes 2097176
  3.5 0.0 copy-start.3
  3.5 0.8 copy-done.3
  4.3 0.0 copy-start.5
  4.3 0.7 copy-done.5
  4.9 0.0 copy-start.1
  5.0 0.0 copy-start.2
  5.0 0.0 copy-start.4
  5.0 1.6 %prepare.1 = (bf16[8,128,1024]{2,1,0:T(8,128)(2,1)S(1)}, bf16[2,16,8,16,256]{4,3,2,1,0:T(8,128)(2,1)S(1)}, s32[64,128]{1,0:T(8,128)S(1)}, bf16[128,128]{1,0:T(8,128)(2,1)S(1)}) custom-call(s32[1]{0:T(128)} %bitcast.h_ref, s32[1,64]{1,0:T(1,128)S(1)} %copy-done.5, s32[1]{0:T(128)S(6)} %copy.11.order_hbm, bf16[128,8192]{1,0:T(8,128)(2,1)S(1)} %copy-done, ...), custom_call_target="tpu_custom_call" | custom-call | tf_op jit(solution)/shard_map/prepare/pallas_call | solution.py:349
  6.5 0.0 copy-done.1
  6.5 0.0 copy-done.2
  6.5 0.0 copy-done.4
  6.6 93.9 %exchange.1 = bf16[128,1024]{1,0:T(8,128)(2,1)S(1)} custom-call(bf16[8,128,1024]{2,1,0:T(8,128)(2,1)S(1)} %get-tuple-element.9.blocks_ref, bf16[2,16,8,16,256]{4,3,2,1,0:T(8,128)(2,1)S(1)} %get-tuple-element.10.panel, s32[64,128]{1,0:T(8,128)S(1)} %get-tuple-element.11.place_ref, bf16[128,128]{1,0:T(8,128)(2,1)S(1)} %get-tuple-element.12.lead, ...), custom_call_target="tpu_custom_call" | custom-call | tf_op jit(solution)/shard_map/exchange/pallas_call | solution.py:369
  100.5 0.7 copy.14
Async XLA Ops:
  1.9 1.6 %copy-start = (bf16[128,8192]{1,0:T(8,128)(2,1)S(1)}, bf16[128,8192]{1,0:T(8,128)(2,1)}, u32[]{:S(2)}) copy-start(bf16[128,8192]{1,0:T(8,128)(2,1)} %front_hbm.1) | copy-start | bytes 6291460
  3.5 0.8 copy-start.3
  4.3 0.7 copy-start.5
  4.9 1.6 %copy-start.1 = (bf16[128,1024]{1,0:T(8,128)(2,1)S(1)}, bf16[128,1024]{1,0:T(8,128)(2,1)}, u32[]{:S(2)}) copy-start(bf16[128,1024]{1,0:T(8,128)(2,1)} %parent.1) | copy-start | bytes 786436
  5.0 1.6 %copy-start.2 = (bf16[256,256]{1,0:T(8,128)(2,1)S(1)}, bf16[256,256]{1,0:T(8,128)(2,1)}, u32[]{:S(2)}) copy-start(bf16[256,256]{1,0:T(8,128)(2,1)} %pinv.1) | copy-start | bytes 393220
  5.0 1.6 %copy-start.4 = (bf16[1,128,128]{2,1,0:T(8,128)(2,1)S(1)}, bf16[1,128,128]{2,1,0:T(8,128)(2,1)}, u32[]{:S(2)}) copy-start(bf16[1,128,128]{2,1,0:T(8,128)(2,1)} %inv.1) | copy-start | bytes 98308
